TPU v7x, 256 devices: a whole 4x4x8 slice. The times are simulated.
256 devices in a mesh: cfg: 2 (over x_lo), seq: 128 (over y, z, x_hi, core).
Axes of the slice: x: 4 (x_hi: 2, x_lo: 2; x = x_hi * 2 + x_lo), y: 4, z: 8, core: 2. Of those that a mesh axis runs over, the one named last changes fastest.
Arguments:
- coarse_hidden: bfloat16 [2, 256, 64, 2048], P('cfg', 'seq'), may hold values from -6 to 6
- coarse_modulation: float32 [2, 2, 2048], P('cfg'), may hold values from -3 to 3
- final_weight: bfloat16 [2048, 32], replicated, may hold values from -0.125 to 0.125
- coarse_latent: float32 [256, 2048], P('seq'), may hold values from -6 to 6
- step_index: int32 [1], replicated, may hold values from 0 to 49
- guide_index: int32 [1], replicated, may hold values from 0 to 4095
- guide_scales: float32 [4096], replicated, may hold values from 1.5 to 6
- upsample_weight: float32 [288, 32], replicated, may hold values from -0.375 to 0.375
- upsample_bias: float32 [32], replicated, may hold values from -3 to 3
- embed_weight: bfloat16 [32, 2048], replicated, may hold values from -1 to 1
- embed_bias: float32 [2048], replicated, may hold values from -3 to 3
- fine_modulation: float32 [3, 2048], replicated, may hold values from -3 to 3
- project_weight: bfloat16 [2048, 3072], P(('cfg', 'seq')), may hold values from -0.125 to 0.125
- query_gain: float32 [128], replicated, may hold values from 0.25 to 1.75
- key_gain: float32 [128], replicated, may hold values from 0.25 to 1.75
- text_keys: bfloat16 [256, 1024], replicated, may hold values from -6 to 6
- text_values: bfloat16 [256, 1024], replicated, may hold values from -6 to 6
- text_length: int32 [1], replicated, may hold values from 192 to 256
- output_weight: bfloat16 [1024, 2048], P(None, ('cfg', 'seq')), may hold values from -0.1875 to 0.1875
Outputs:
- guided_velocity: float32 [256, 2048], P('seq')
- fine_latent: float32 [256, 2, 4096], P('seq', 'cfg')
- fine_hidden: bfloat16 [256, 2, 128, 2048], P('seq', 'cfg')
All inputs are finite; a program needn't handle non-finite values.
Results may differ from a plain program's by a relative error of at most 0.0053.
Values may be sent and summed in bfloat16 or wider, within the bound.
A program may use at most 128 MiB of HBM per device.

v0:
```python
import jax
import jax.numpy as jnp
from jax import lax
from jax.sharding import PartitionSpec as P

HEADS = 8
STEPS = 50
epsilon = 1e-06
flow_shift = 5.0
highest = lax.Precision.HIGHEST


def from_partner(shard, axis, bit):
    return lax.ppermute(shard, axis, [(i, i ^ 1 << bit) for i in range(lax.axis_size(axis))])


def with_halo(block, sides, width):
    for axis, dim in sides:
        count = lax.axis_size(axis)
        forward = [(i, i + 1) for i in range(count - 1)]
        backward = [(target, source) for source, target in forward]
        low = lax.ppermute(
            lax.slice_in_dim(block, block.shape[dim] - width, None, axis=dim), axis, forward
        )
        high = lax.ppermute(lax.slice_in_dim(block, 0, width, axis=dim), axis, backward)
        block = jnp.concatenate([low, block, high], axis=dim)
    return block


def layer_norm(values):
    centred = values - jnp.mean(values, -1, keepdims=True)
    return centred * lax.rsqrt(jnp.mean(centred * centred, -1, keepdims=True) + epsilon)


def rms_heads(values, gain_vector, head_width):
    shaped = values.reshape(values.shape[0], -1, head_width)
    scaled = (
        shaped * lax.rsqrt(jnp.mean(shaped * shaped, -1, keepdims=True) + epsilon) * gain_vector
    )
    return scaled.reshape(values.shape[0], -1)


def sigma_at(step_value):
    fraction = 1.0 - step_value.astype(jnp.float32) / STEPS
    return flow_shift * fraction / (1.0 + (flow_shift - 1.0) * fraction)


def pick_scale(scale_table, slot_index):
    slots = jnp.arange(scale_table.shape[0], dtype=jnp.int32)
    return jnp.sum(jnp.where(slots == slot_index, scale_table, 0.0))


def attend(queries, image_keys, image_values, text_keys, text_values, image_mask, text_mask, heads):
    head_width = queries.shape[1] // heads
    score_scale = head_width ** (-0.5)
    dims = (((1,), (1,)), ((), ()))

    def one_head(head_index):
        column_start = head_index * head_width
        query_part = lax.dynamic_slice_in_dim(queries, column_start, head_width, 1)
        key_part = lax.dynamic_slice_in_dim(image_keys, column_start, head_width, 1)
        value_part = lax.dynamic_slice_in_dim(image_values, column_start, head_width, 1)
        text_key_part = lax.dynamic_slice_in_dim(text_keys, column_start, head_width, 1)
        text_value_part = lax.dynamic_slice_in_dim(text_values, column_start, head_width, 1)
        image_scores = (
            lax.dot_general(query_part, key_part, dims, preferred_element_type=jnp.float32)
            * score_scale
        )
        text_scores = (
            lax.dot_general(query_part, text_key_part, dims, preferred_element_type=jnp.float32)
            * score_scale
        )
        image_weights = jnp.where(image_mask, jnp.exp(image_scores), 0.0)
        text_weights = jnp.where(text_mask, jnp.exp(text_scores), 0.0)
        denominator = jnp.sum(image_weights, 1, keepdims=True) + jnp.sum(
            text_weights, 1, keepdims=True
        )
        image_weights = (image_weights / denominator).astype(jnp.bfloat16)
        text_weights = (text_weights / denominator).astype(jnp.bfloat16)
        return jnp.dot(image_weights, value_part, preferred_element_type=jnp.float32) + jnp.dot(
            text_weights, text_value_part, preferred_element_type=jnp.float32
        )

    stacked = lax.map(one_head, jnp.arange(heads, dtype=jnp.int32))
    return stacked.transpose(1, 0, 2).reshape(queries.shape[0], -1).astype(jnp.bfloat16)


def conv_rows(above, centre, below, upsample_weight, upsample_bias):
    tap_list = []
    for row_set in (above, centre, below):
        breadth = row_set.shape[1]
        padded = jnp.pad(row_set, ((0, 0), (1, 1), (0, 0)))
        for col_shift in range(3):
            tap_list.append(padded[:, col_shift : col_shift + breadth])
    patches = jnp.concatenate(tap_list, -1)
    flat_patches = patches.reshape(-1, patches.shape[-1])
    product = jnp.dot(flat_patches, upsample_weight, precision=highest).reshape(centre.shape)
    return product + upsample_bias + centre


def per_device(
    coarse_hidden,
    coarse_modulation,
    final_weight,
    coarse_latent,
    step_index,
    guide_index,
    guide_scales,
    upsample_weight,
    upsample_bias,
    embed_weight,
    embed_bias,
    fine_modulation,
    project_weight,
    query_gain,
    key_gain,
    text_keys,
    text_values,
    text_length,
    output_weight,
):
    row_count = coarse_hidden.shape[1]
    row_cells = coarse_hidden.shape[2]
    model_width = coarse_hidden.shape[3]
    channels = final_weight.shape[1]
    head_width = query_gain.shape[0]
    inner = project_weight.shape[1] // 3
    reach = max(row_count // 2, 1)
    branch = lax.axis_index("cfg")
    seq_index = lax.axis_index("seq")
    normed = layer_norm(coarse_hidden[0].astype(jnp.float32))
    modulated = (normed * (1.0 + coarse_modulation[0, 1]) + coarse_modulation[0, 0]).astype(
        jnp.bfloat16
    )
    velocity = jnp.dot(
        modulated.reshape(row_count * row_cells, model_width),
        final_weight,
        preferred_element_type=jnp.float32,
    ).reshape(row_count, row_cells * channels)
    partner = from_partner(velocity, "cfg", 0)
    conditional = jnp.where(branch == 0, velocity, partner)
    unconditional = jnp.where(branch == 0, partner, velocity)
    guidance = pick_scale(guide_scales, guide_index[0])
    guided = unconditional + guidance * (conditional - unconditional)
    stepped = coarse_latent + (sigma_at(step_index[0] + 1) - sigma_at(step_index[0])) * guided
    scale = 1.0 + fine_modulation[1]
    embed32 = embed_weight.astype(jnp.float32)
    embed_centred = embed32 - jnp.mean(embed32, -1, keepdims=True)
    bias_centred = embed_bias - jnp.mean(embed_bias)
    folded_left = jnp.concatenate(
        [embed_centred * scale, (bias_centred * scale)[None], fine_modulation[0][None]], 0
    )
    depth = project_weight.shape[0]
    device = branch * lax.axis_size("seq") + seq_index
    left_part = lax.dynamic_slice_in_dim(folded_left, device * depth, depth, 1)
    folded = lax.psum(
        jnp.dot(left_part, project_weight.astype(jnp.float32), precision=highest), ("cfg", "seq")
    )
    output_rows = lax.all_gather(output_weight.T, ("cfg", "seq"), axis=0, tiled=True)

    def embed_rows(grid_rows):
        grid_tokens = grid_rows.reshape(-1, channels).astype(jnp.bfloat16)
        centred = (
            jnp.dot(grid_tokens.astype(jnp.float32), embed_centred, precision=highest)
            + bias_centred
        )
        rstd = lax.rsqrt(jnp.mean(centred * centred, -1, keepdims=True) + epsilon)
        return (grid_tokens, rstd)

    def project(tokens_rstd, start, stop):
        tokens, rstd = tokens_rstd
        part = folded[:, start:stop]
        product = jnp.dot(tokens.astype(jnp.float32), part[:channels], precision=highest)
        return rstd * (product + part[channels]) + part[channels + 1]

    latent_grid = stepped.reshape(row_count, row_cells, channels)
    rim_width = reach + 1
    rimmed = with_halo(latent_grid, (("seq", 0),), rim_width)
    upsampled = jnp.repeat(jnp.repeat(rimmed, 2, 0), 2, 1)
    span = row_count + 2 * reach
    wide_grid = conv_rows(
        upsampled[1 : 1 + 2 * span],
        upsampled[2 : 2 + 2 * span],
        upsampled[3 : 3 + 2 * span],
        upsample_weight,
        upsample_bias,
    )
    grouped = wide_grid.reshape(span, 2, 2 * row_cells, channels)
    fine_grid = lax.dynamic_index_in_dim(
        grouped[reach : reach + row_count], branch, 1, keepdims=False
    )
    own = embed_rows(fine_grid)
    fine_state = jnp.dot(own[0], embed_weight, preferred_element_type=jnp.float32) + embed_bias
    around = embed_rows(wide_grid)
    token_count = own[0].shape[0]
    query_sum = project(own, 0, inner)
    key_sum = project(around, inner, 2 * inner)
    value_sum = project(around, 2 * inner, 3 * inner)
    queries = rms_heads(query_sum, query_gain, head_width).astype(jnp.bfloat16)
    keys = rms_heads(key_sum, key_gain, head_width).astype(jnp.bfloat16)
    values = value_sum.astype(jnp.bfloat16)
    image_keys, image_values = (keys, values)
    normed_text_keys = rms_heads(text_keys.astype(jnp.float32), key_gain, head_width).astype(
        jnp.bfloat16
    )
    key_count = image_keys.shape[0]
    query_rows = jnp.arange(token_count, dtype=jnp.int32) // (2 * row_cells)
    key_rows = jnp.arange(key_count, dtype=jnp.int32) // (4 * row_cells)
    distance = key_rows[None, :] - query_rows[:, None]
    global_rows = seq_index * row_count + key_rows - reach
    row_valid = (global_rows >= 0) & (global_rows < row_count * lax.axis_size("seq"))
    image_mask = (distance >= 0) & (distance <= 2 * reach) & row_valid[None, :]
    text_mask = (jnp.arange(text_keys.shape[0], dtype=jnp.int32) < text_length[0])[None, :]
    attended = attend(
        queries,
        image_keys,
        image_values,
        normed_text_keys,
        text_values,
        image_mask,
        text_mask,
        HEADS,
    )
    output_part = lax.dot_general(
        attended, output_rows, (((1,), (1,)), ((), ())), preferred_element_type=jnp.float32
    )
    fine_hidden = (fine_state + fine_modulation[2] * output_part).astype(jnp.bfloat16)
    fine_hidden = fine_hidden.reshape(row_count, 1, 2 * row_cells, model_width)
    fine_latent = fine_grid.reshape(row_count, 1, 2 * row_cells * channels)
    return (guided, fine_latent, fine_hidden)


def solution(mesh):
    placed = (
        P("cfg", "seq", None, None),
        P("cfg", None, None),
        P(),
        P("seq", None),
        P(),
        P(),
        P(),
        P(),
        P(),
        P(),
        P(),
        P(),
        P(("cfg", "seq"), None),
        P(),
        P(),
        P(),
        P(),
        P(),
        P(None, ("cfg", "seq")),
    )
    return jax.shard_map(
        per_device,
        mesh=mesh,
        in_specs=placed,
        out_specs=(P("seq", None), P("seq", "cfg", None), P("seq", "cfg", None, None)),
        check_vma=False,
    )
```

profile of v0, /device:TPU:32, one launch (start us, length us, event | category | flops | bytes accessed | tf_op | source)
XLA Modules:
  0.0 696.4 jit_solution(8204464123050728577)
XLA Ops:
  7.3 1.5 fusion.84
  10.8 1.3 reduce_sum.112
  13.5 2.0 fusion.65
  17.0 1.6 collective-permute-start
  23.5 1.3 multiply_add_fusion.1
  24.9 1.9 collective-permute-start.1
  27.4 6.0 collective-permute-start.2
  33.5 1.8 collective-permute-done.2
  39.3 1.2 fusion.28
  40.4 4.5 multiply_reduce_fusion
  45.0 223.4 %all-reduce.5.cloned.1.call-done = f32[34,3072]{1,0:T(8,128)} async-done(((f32[34,3072]{1,0:T(8,128)}), f32[34,3072]{1,0:T(8,128)}) %all-reduce.5.cloned.1.call-update) | async-done | bytes 417808 | tf_op jit(solution)/shard_map/psum | solution.py:156
  269.3 1.6 fusion.30
  271.7 3.4 bitcast_reduce_fusion
  275.9 1.1 fusion.23
  277.0 4.4 add_convert_fusion
  281.9 58.2 %while.11 = (s32[]{:T(128)}, bf16[8,256,128]{1,2,0:T(8,128)(2,1)}, s32[8]{0:T(128)}, bf16[256,1024]{1,0:T(8,128)(2,1)S(1)}, bf16[1024,1024]{0,1:T(8,128)(2,1)S(1...) while((s32[]{:T(128)}, bf16[8,256,128]{1,2,0:T(8,128)(2,1)}, ...), condition=%wide.region_14.15_spmd.clone, body=%wide.region_11.14_spmd.clone.sunk | while | flops 170786816 | bytes 4014055 | solution.py:84
  281.9 1.2 dynamic_slice.86
  284.7 1.3 fusion.102
  286.0 1.1 fusion.103
  287.1 1.3 fusion.104
  289.2 1.2 dynamic_slice.86
  291.9 1.3 fusion.102
  293.3 1.1 fusion.103
  294.3 1.3 fusion.104
  296.4 1.2 dynamic_slice.86
  299.2 1.3 fusion.102
  301.6 1.3 fusion.104
  303.7 1.2 dynamic_slice.86
  306.5 1.3 fusion.102
  308.9 1.3 fusion.104
  311.0 1.2 dynamic_slice.86
  313.8 1.3 fusion.102
  315.1 1.1 fusion.103
  316.2 1.3 fusion.104
  318.3 1.2 dynamic_slice.86
  321.0 1.3 fusion.102
  323.4 1.3 fusion.104
  325.5 1.2 dynamic_slice.86
  328.3 1.3 fusion.102
  329.6 1.1 fusion.103
  330.7 1.3 fusion.104
  332.8 1.2 dynamic_slice.86
  335.6 1.3 fusion.102
  336.9 1.1 fusion.103
  338.0 1.3 fusion.104
  340.1 344.3 %all-gather.2.cloned.1.call-done = bf16[2048,1024]{1,0:T(8,128)(2,1)} async-done(((bf16[8,1024]{1,0:T(8,128)(2,1)}), bf16[2048,1024]{1,0:T(8,128)(2,1)}) %all-gather.2.cloned.1.call-update) | async-done | bytes 4194320 | tf_op jit(solution)/shard_map/all_gather | solution.py:159
  684.4 3.6 convolution_multiply_fusion.2
  688.1 1.4 fusion.27
  (153 shorter events, 31.5 us)
Async XLA Ops:
  7.2 9.5 %copy-start = (bf16[2048,32]{0,1:T(8,128)(2,1)S(1)}, bf16[2048,32]{0,1:T(8,128)(2,1)}, u32[]{:S(2)}) copy-start(bf16[2048,32]{0,1:T(8,128)(2,1)} %param.23) | copy-start | bytes 393220
  7.2 8.4 %copy-start.1 = (bf16[1,2,64,2048]{3,2,1,0:T(8,128)(2,1)S(1)}, bf16[1,2,64,2048]{3,2,1,0:T(8,128)(2,1)}, u32[]{:S(2)}) copy-start(bf16[1,2,64,2048]{3,2,1,0:T(8,128)(2,1)} %param.21) | copy-start | bytes 1572868
  7.2 8.9 %copy-start.8 = (f32[1,2,2048]{2,1,0:T(2,128)S(1)}, f32[1,2,2048]{2,1,0:T(2,128)}, u32[]{:S(2)}) copy-start(f32[1,2,2048]{2,1,0:T(2,128)} %param.22) | copy-start | bytes 49156
  7.2 261.2 %all-reduce.5.cloned.1.call-start = ((), (), s32[]{:S(2)}) async-start(), calls=%async_computation | async-start | bytes 983040 | tf_op jit(solution)/shard_map/psum | solution.py:156
  13.4 6.4 copy-start.12
  13.5 6.5 copy-start.13
  13.5 6.5 copy-start.2
  15.5 668.9 %all-gather.2.cloned.1.call-start = ((), (), s32[]{:S(2)}) async-start(), calls=%async_computation.1 | async-start | bytes 4210688 | tf_op jit(solution)/shard_map/all_gather | solution.py:159
  17.0 6.4 collective-permute-start
  20.1 0.8 copy-start.9
  20.6 2.9 copy-start.10
  24.9 8.6 %collective-permute-start.1 = (f32[2,64,32]{2,1,0:T(8,128)S(1)}, f32[2,64,32]{2,1,0:T(8,128)S(1)}, u32[]{:S(2)}, u32[]{:S(2)}) collective-permute-start(f32[2,64,32]{2,1,0:T(8,128)S(1)} %reshape.230), channel_id=1, source_target_pairs={{0,1},{1,2},{2,3},{3,4},{4,5},{5,6},{6,7},{7,8},{8,9},{9,10},{10,1... | collective-permute-start | bytes 49160 | tf_op jit(solution)/shard_map/ppermute | solution.py:22
  27.4 7.9 %collective-permute-start.2 = (f32[2,64,32]{2,1,0:T(8,128)S(1)}, f32[2,64,32]{2,1,0:T(8,128)S(1)}, u32[]{:S(2)}, u32[]{:S(2)}) collective-permute-start(f32[2,64,32]{2,1,0:T(8,128)S(1)} %reshape.230), channel_id=1, source_target_pairs={{1,0},{2,1},{3,2},{4,3},{5,4},{6,5},{7,6},{8,7},{9,8},{10,9},{11,1... | collective-permute-start | bytes 49160 | tf_op jit(solution)/shard_map/ppermute | solution.py:25
  36.3 1.1 copy-start.7
  36.3 1.1 copy-start.11
  36.9 2.3 copy-start.3
  38.4 233.4 %copy-start.5 = (bf16[8,4,8,128]{3,2,1,0:T(8,128)(2,1)}, bf16[8,4,8,128]{3,2,1,0:T(8,128)(2,1)S(1)}, u32[]{:S(2)}) copy-start(bf16[8,4,8,128]{3,2,1,0:T(8,128)(2,1)S(1)} %convert_bitcast_fusion) | copy-start | bytes 196612
  275.9 1.1 copy-start.6
  684.4 3.6 copy-start.4
Sparse Core Ops, SparseCore 0:
  15.6 252.6 all-reduce.4
  270.3 414.1 all-gather.1
where the time goes:
time: 698 us; the launch traced here: 696 us
  waiting for transfers between devices  570 us (82%)
  matrix products  55 us (8%)
  local copies, waits for them, and re-layouts  21.8 us (3%)
  other arithmetic  18.2 us (3%)
  between operations  16.7 us (2%)
  starting transfers between devices  9.61 us (1%)
    all_gather x1, waiting for transfers between devices, per_device(): lax.all_gather(output_weight.T, ('cfg', 'seq'), axis=0, tiled=True)  344 us
    psum x1, waiting for transfers between devices, per_device(): lax.psum(jnp.dot(left_part, project_weight.astype(jnp.float32), precision...  223 us
  transfers between devices with their start and end apart: 5, of which 3 were waited for; matrix products, arithmetic and copies ran while one was open for 12% of the time, Pallas kernels for 0%

commit v1 on v0

--- a/solution.py
+++ b/solution.py
@@ -8,6 +8,13 @@
 epsilon = 1e-06
 flow_shift = 5.0
 highest = lax.Precision.HIGHEST
+
+
+def all_by_exchange(x, axis, d):
+    size = lax.axis_size(axis)
+    blocks = jnp.stack([x for _ in range(size)])
+    blocks = lax.all_to_all(blocks, axis, split_axis=0, concat_axis=0)
+    return jnp.concatenate(blocks, axis=d)
 
 
 def from_partner(shard, axis, bit):
@@ -156,7 +163,7 @@
     folded = lax.psum(
         jnp.dot(left_part, project_weight.astype(jnp.float32), precision=highest), ("cfg", "seq")
     )
-    output_rows = lax.all_gather(output_weight.T, ("cfg", "seq"), axis=0, tiled=True)
+    output_rows = all_by_exchange(output_weight.T, ("cfg", "seq"), 0)
 
     def embed_rows(grid_rows):
         grid_tokens = grid_rows.reshape(-1, channels).astype(jnp.bfloat16)

time: 698 us -> 376 us (0.54)
  waiting for transfers between devices: 570 us -> 229 us
  starting transfers between devices: 9.61 us -> 24.7 us
    all_gather x1 -> x0, waiting for transfers between devices: 344 us -> none  [per_device(): lax.all_gather(output_weight.T, ('cfg', 'seq'), axis=0, tiled=True)]
    ppermute x1, waiting for transfers between devices: 0.01 us -> 75.9 us  [with_halo(): lax.ppermute(lax.slice_in_dim(block, block.shape[dim] - width, None, axis...]
    psum x1, waiting for transfers between devices: 223 us -> 153 us  [per_device(): lax.psum(jnp.dot(left_part, project_weight.astype(jnp.float32), precision...]
    all_to_all x0 -> x1, starting transfers between devices: none -> 15.1 us  [all_by_exchange(): blocks = lax.all_to_all(blocks, axis, split_axis=0, concat_axis=0)]
  transfers between devices with their start and end apart: 5 -> 5, of which waited for: 3 -> 2; matrix products, arithmetic and copies ran while one was open for 12% -> 23% of each run, Pallas kernels for 0% -> 0%
where the time goes in v1:
time: 376 us; the launch traced here: 371 us
  waiting for transfers between devices  229 us (61%)
  matrix products  54.4 us (14%)
  starting transfers between devices  24.7 us (7%)
  local copies, waits for them, and re-layouts  24.3 us (6%)
  other arithmetic  18 us (5%)
  between operations  16.7 us (4%)
  loops' own time  4.72 us (1%)
    psum x1, waiting for transfers between devices, per_device(): lax.psum(jnp.dot(left_part, project_weight.astype(jnp.float32), precision...  153 us
    ppermute x1, waiting for transfers between devices, with_halo(): lax.ppermute(lax.slice_in_dim(block, block.shape[dim] - width, None, axis...  75.9 us
    all_to_all x1, starting transfers between devices, all_by_exchange(): blocks = lax.all_to_all(blocks, axis, split_axis=0, concat_axis=0)  15.1 us
    dot_general x8, matrix products, one_head(): jnp.dot(image_weights, value_part, preferred_element_type=jnp.float32)  10.6 us
    dot_general x8, matrix products, one_head(): lax.dot_general(query_part, key_part, dims, preferred_element_type=jnp.fl...  10.6 us
    dynamic_slice x8, local copies, waits for them, and re-layouts, attend(): stacked = lax.map(one_head, jnp.arange(heads, dtype=jnp.int32))  9.71 us
    dot_general x3, matrix products, project(): jnp.dot(tokens.astype(jnp.float32), part[:channels], precision=highest)  9.45 us
    dot_general x8, matrix products, one_head(): jnp.dot(text_weights, text_value_part, preferred_element_type=jnp.float32)  8.64 us
  transfers between devices with their start and end apart: 5, of which 2 were waited for; matrix products, arithmetic and copies ran while one was open for 23% of the time, Pallas kernels for 0%

profile of v1, /device:TPU:32, one launch (start us, length us, event | category | flops | bytes accessed | tf_op | source)
XLA Modules:
  0.0 371.4 jit_solution(17636255506332269571)
XLA Ops:
  7.3 1.3 convert_reduce_fusion
  8.6 1.3 fusion.43
  10.9 1.4 fusion.47
  12.7 1.6 collective-permute-start
  16.5 1.3 fusion.70
  17.7 2.5 stack.2
  20.3 15.1 %all-to-all-start = ((bf16[256,8,1024]{2,1,0:T(8,128)(2,1)}), bf16[256,8,1024]{2,1,0:T(8,128)(2,1)}, u32[]{:S(2)}, u32[]{:S(2)}) async-start(bf16[256,8,1024]{2,1,0:T(8,128)(2,1)} %stack.2), calls=%async_computation | async-start | bytes 8388608 | tf_op jit(solution)/shard_map/all_to_all | solution.py:16
  40.1 1.3 multiply_add_fusion.1
  41.5 2.1 collective-permute-start.1
  44.1 5.9 %collective-permute-start.2 = (f32[2,64,32]{2,1,0:T(8,128)S(1)}, f32[2,64,32]{2,1,0:T(8,128)S(1)}, u32[]{:S(2)}, u32[]{:S(2)}) collective-permute-start(f32[2,64,32]{2,1,0:T(8,128)S(1)} %reshape.235), channel_id=1, source_target_pairs={{1,0},{2,1},{3,2},{4,3},{5,4},{6,5},{7,6},{8,7},{9,8},{10,9},{11,1... | collective-permute-start | bytes 49160 | tf_op jit(solution)/shard_map/ppermute | solution.py:32
  50.0 75.9 %collective-permute-done.1 = f32[2,64,32]{2,1,0:T(8,128)S(1)} collective-permute-done((f32[2,64,32]{2,1,0:T(8,128)S(1)}, f32[2,64,32]{2,1,0:T(8,128)S(1)}, u32[]{:S(2)}, u32[]{:S(2)}) %collective-permute-start.1) | collective-permute-done | bytes 16416 | tf_op jit(solution)/shard_map/ppermute | solution.py:29
  129.9 1.2 fusion.33
  131.0 4.5 %multiply_reduce_fusion = f32[1024]{0:T(1024)S(1)} fusion(f32[2048]{0:T(1024)S(1)} %get-tuple-element.189, bf16[32,2048]{1,0:T(8,128)(2,1)S(1)} %copy-done.2, f32[32]{0:T(128)S(1)} %broadcast_multiply_fusion.1, bf16[8,4,8,128]{3,2,1,0:T(8,128)(2,1)S(1)} %convert_bitcast_fusion), kind=kOutput, calls=%fused_computation.29 | convolution fusion | flops 811727872 | bytes 209024 | tf_op jit(solution)/shard_map/dot_general | solution.py:171
  135.6 152.7 %all-reduce.5.cloned.1.call-done = f32[34,3072]{1,0:T(8,128)} async-done(((f32[34,3072]{1,0:T(8,128)}), f32[34,3072]{1,0:T(8,128)}) %all-reduce.5.cloned.1.call-update) | async-done | bytes 417808 | tf_op jit(solution)/shard_map/psum | solution.py:163
  289.2 1.6 fusion.35
  291.6 3.4 bitcast_reduce_fusion
  295.8 1.1 fusion.25
  296.9 4.4 %add_convert_fusion = bf16[1024,1024]{0,1:T(8,128)(2,1)} fusion(f32[1024]{0:T(1024)S(1)} %bitcast.147, f32[1024]{0:T(1024)S(1)} %bitcast.146, f32[1024]{0:T(1024)S(1)} %add_rsqrt_fusion.3, f32[34,3072]{1,0:T(8,128)} %all-reduce.5.cloned.1.call-done, bf16[8,4,8,128]{3,2,1,0:T(8,128)(2,1)S(1)} %copy-done.6), kind=kOutput, calls=%fused_computation.36 | convolution fusion | flops 406847488 | bytes 2306048 | tf_op jit(solution)/shard_map/dot_general | solution.py:180
  301.9 57.6 %while.11 = (s32[]{:T(128)}, bf16[8,256,128]{1,2,0:T(8,128)(2,1)}, s32[8]{0:T(128)}, bf16[256,1024]{1,0:T(8,128)(2,1)S(1)}, bf16[1024,1024]{0,1:T(8,128)(2,1)S(1...) while((s32[]{:T(128)}, bf16[8,256,128]{1,2,0:T(8,128)(2,1)}, ...), condition=%wide.region_14.15_spmd.clone, body=%wide.region_11.14_spmd.clone.sunk | while | flops 170786816 | bytes 4014055 | solution.py:91
  301.9 1.2 dynamic_slice.86
  304.6 1.3 fusion.106
  305.9 1.1 fusion.107
  307.0 1.3 fusion.108
  309.1 1.2 dynamic_slice.86
  311.8 1.3 fusion.106
  313.1 1.1 fusion.107
  314.2 1.3 fusion.108
  316.3 1.2 dynamic_slice.86
  319.0 1.3 fusion.106
  321.4 1.3 fusion.108
  323.5 1.2 dynamic_slice.86
  326.2 1.3 fusion.106
  328.6 1.3 fusion.108
  330.7 1.2 dynamic_slice.86
  333.4 1.3 fusion.106
  335.8 1.3 fusion.108
  337.9 1.2 dynamic_slice.86
  340.6 1.3 fusion.106
  341.9 1.1 fusion.107
  343.0 1.3 fusion.108
  345.1 1.2 dynamic_slice.86
  347.8 1.3 fusion.106
  350.2 1.3 fusion.108
  352.3 1.2 dynamic_slice.86
  355.0 1.3 fusion.106
  357.4 1.3 fusion.108
  359.5 3.6 fusion.27
  363.1 1.4 fusion.32
  (157 shorter events, 32.2 us)
Async XLA Ops:
  7.2 5.2 %copy-start = (bf16[2048,32]{0,1:T(8,128)(2,1)S(1)}, bf16[2048,32]{0,1:T(8,128)(2,1)}, u32[]{:S(2)}) copy-start(bf16[2048,32]{0,1:T(8,128)(2,1)} %param.23) | copy-start | bytes 393220
  7.2 7.1 %copy-start.9 = (f32[3,2048]{1,0:T(4,128)S(1)}, f32[3,2048]{1,0:T(4,128)}, u32[]{:S(2)}) copy-start(f32[3,2048]{1,0:T(4,128)} %param.32) | copy-start | bytes 73732
  7.2 7.7 %copy-start.2 = (bf16[32,2048]{1,0:T(8,128)(2,1)S(1)}, bf16[32,2048]{1,0:T(8,128)(2,1)}, u32[]{:S(2)}) copy-start(bf16[32,2048]{1,0:T(8,128)(2,1)} %param.30) | copy-start | bytes 393220
  7.2 8.0 %copy-start.3 = (f32[2048]{0:T(1024)S(1)}, f32[2048]{0:T(1024)}, u32[]{:S(2)}) copy-start(f32[2048]{0:T(1024)} %param.31) | copy-start | bytes 24580
  7.2 9.2 %copy-start.8 = (bf16[8,3072]{1,0:T(8,128)(2,1)S(1)}, bf16[8,3072]{1,0:T(8,128)(2,1)}, u32[]{:S(2)}) copy-start(bf16[8,3072]{1,0:T(8,128)(2,1)} %param.33) | copy-start | bytes 147460
  7.2 281.1 %all-reduce.5.cloned.1.call-start = ((), (), s32[]{:S(2)}) async-start(), calls=%async_computation.1 | async-start | bytes 983040 | tf_op jit(solution)/shard_map/psum | solution.py:163
  8.6 9.2 %copy-start.10 = (bf16[1024,8]{0,1:T(8,128)(2,1)S(1)}, bf16[1024,8]{0,1:T(8,128)(2,1)}, u32[]{:S(2)}) copy-start(bf16[1024,8]{0,1:T(8,128)(2,1)} %param.39) | copy-start | bytes 49156
  12.7 27.4 %collective-permute-start = (f32[2,2048]{1,0:T(2,128)S(1)}, f32[2,2048]{1,0:T(2,128)S(1)}, u32[]{:S(2)}, u32[]{:S(2)}) collective-permute-start(f32[2,2048]{1,0:T(2,128)S(1)} %reshape.234), channel_id=1, source_target_pairs={{0,128},{128,0},{1,129},{129,1},{2,130},{130,2},{3,131},{131,3},{4... | collective-permute-start | bytes 49160 | tf_op jit(solution)/shard_map/ppermute | solution.py:21
  20.2 16.4 %copy-start.14 = (f32[128]{0:T(128)S(1)}, f32[128]{0:T(128)}, u32[]{:S(2)}) copy-start(f32[128]{0:T(128)} %param.34) | copy-start | bytes 1540
  20.2 16.4 %copy-start.15 = (f32[128]{0:T(128)S(1)}, f32[128]{0:T(128)}, u32[]{:S(2)}) copy-start(f32[128]{0:T(128)} %param.35) | copy-start | bytes 1540
  20.2 16.4 %copy-start.1 = (bf16[256,1024]{1,0:T(8,128)(2,1)S(1)}, bf16[256,1024]{1,0:T(8,128)(2,1)}, u32[]{:S(2)}) copy-start(bf16[256,1024]{1,0:T(8,128)(2,1)} %param.36) | copy-start | bytes 1572868
  20.3 339.2 %all-to-all-start = ((bf16[256,8,1024]{2,1,0:T(8,128)(2,1)}), bf16[256,8,1024]{2,1,0:T(8,128)(2,1)}, u32[]{:S(2)}, u32[]{:S(2)}) async-start(bf16[256,8,1024]{2,1,0:T(8,128)(2,1)} %stack.2), calls=%async_computation | async-start | bytes 8388608 | tf_op jit(solution)/shard_map/all_to_all | solution.py:16
  36.8 0.8 copy-start.11
  37.3 2.8 copy-start.12
  41.5 84.4 %collective-permute-start.1 = (f32[2,64,32]{2,1,0:T(8,128)S(1)}, f32[2,64,32]{2,1,0:T(8,128)S(1)}, u32[]{:S(2)}, u32[]{:S(2)}) collective-permute-start(f32[2,64,32]{2,1,0:T(8,128)S(1)} %reshape.235), channel_id=1, source_target_pairs={{0,1},{1,2},{2,3},{3,4},{4,5},{5,6},{6,7},{7,8},{8,9},{9,10},{10,1... | collective-permute-start | bytes 49160 | tf_op jit(solution)/shard_map/ppermute | solution.py:29
  44.1 81.8 %collective-permute-start.2 = (f32[2,64,32]{2,1,0:T(8,128)S(1)}, f32[2,64,32]{2,1,0:T(8,128)S(1)}, u32[]{:S(2)}, u32[]{:S(2)}) collective-permute-start(f32[2,64,32]{2,1,0:T(8,128)S(1)} %reshape.235), channel_id=1, source_target_pairs={{1,0},{2,1},{3,2},{4,3},{5,4},{6,5},{7,6},{8,7},{9,8},{10,9},{11,1... | collective-permute-start | bytes 49160 | tf_op jit(solution)/shard_map/ppermute | solution.py:32
  126.9 1.1 copy-start.7
  126.9 1.1 copy-start.13
  129.0 162.7 %copy-start.5 = (bf16[8,4,8,128]{3,2,1,0:T(8,128)(2,1)}, bf16[8,4,8,128]{3,2,1,0:T(8,128)(2,1)S(1)}, u32[]{:S(2)}) copy-start(bf16[8,4,8,128]{3,2,1,0:T(8,128)(2,1)S(1)} %convert_bitcast_fusion) | copy-start | bytes 196612
  295.8 1.1 copy-start.6
  359.5 3.6 copy-start.4
Sparse Core Ops, SparseCore 0:
  17.9 270.3 all-reduce.4
